TPU v7x, 512 devices: a whole 4x8x8 slice. The times are simulated.
512 devices in a mesh: batch: 2 (over core), token: 32 (over x, z), hidden: 8 (over y).
Axes of the slice: x: 4, y: 8, z: 8, core: 2. Of those that a mesh axis runs over, the one named last changes fastest.
Arguments:
- hist_len: int32 [512], replicated, may hold values from 32 to 512, as said below
- queries: bfloat16 [32, 1536], P(None, 'token'), may hold values from -4 to 4
- history_keys: bfloat16 [1536, 1536, 128], P(('batch', 'hidden'), 'token'), may hold values from -192 to 192
- cached_history_values: bfloat16 [1536, 1536, 128], P(('batch', 'hidden'), 'token'), may hold values from -6 to 6
- gain_mix: float32 [1536], replicated, may hold values from 0.25 to 1.75
- w_up: bfloat16 [32, 1536, 3072], P('token', None, 'hidden'), may hold values from -0.15625 to 0.15625
- w_down: bfloat16 [32, 3072, 1536], P('token', 'hidden'), may hold values from -0.109375 to 0.109375
- gain_out: float32 [1536], replicated, may hold values from 0.25 to 1.75
Outputs:
- mixer_out: bfloat16 [512, 32, 1536], P(('batch', 'hidden'), 'token')
Inputs may be any that keep to these rules, and one draw needn't show every extreme that they name: `hist_len`: along batch+hidden, the requests of each index need between 32 and 96 slots, indices 2i and 2i + 1 need 4 * 32 slots together, and some index needs exactly 96; within an index, requests 2j and 2j + 1 need from 2 to 6 slots together.
All inputs are finite; a program needn't handle non-finite values.
Results may differ from a plain program's by a relative error of at most 0.015.
Values may be sent and summed in bfloat16 or wider, within the bound.
A program may use at most 64 MiB of HBM per device.

v0:
```python
import jax
import jax.numpy as jnp
from jax import lax
from jax.sharding import PartitionSpec as P

TOKEN_COUNT = 32
MODEL_WIDTH = 1536
BLOCK_POSITIONS = 128
REQ_DEV = 32
EPSILON = 1e-05
NEGATIVE_FILL = -1e30


def in_blocks(x, dim, length):
    dims = x.shape
    parts = x.reshape(*dims[:dim], length, dims[dim] // length, *dims[dim + 1 :])
    return jnp.moveaxis(parts, dim, 0)


def sent_and_summed(x, axis, dim):
    length = lax.axis_size(axis)
    parts = lax.all_to_all(in_blocks(x, dim, length), axis, 0, 0, tiled=True)
    return jnp.sum(parts.astype(jnp.float32), axis=0)


def slot_layout(lengths, slot_count, block_rows):
    request_count = lengths.shape[0]
    blocks = (lengths + block_rows - 1) // block_rows
    block_ends = jnp.cumsum(blocks)
    block_starts = block_ends - blocks
    slot_index = jnp.arange(slot_count, dtype=jnp.int32)
    owners = jnp.sum((block_ends[None, :] <= slot_index[:, None]).astype(jnp.int32), axis=1)
    onehot = owners[:, None] == jnp.arange(request_count, dtype=jnp.int32)[None, :]
    start_of = jnp.sum(jnp.where(onehot, block_starts[None, :], 0), axis=1)
    length_of = jnp.sum(jnp.where(onehot, lengths[None, :], 0), axis=1)
    valid_rows = jnp.clip(length_of - (slot_index - start_of) * block_rows, 0, block_rows)
    return (onehot, valid_rows)


def block_partials(query_heads, slot_keys, slot_values, valid_rows, score_scale):
    scores = (
        jnp.einsum("qhs,nhsp->nqhp", query_heads, slot_keys, preferred_element_type=jnp.float32)
        * score_scale
    )
    position = jnp.arange(slot_keys.shape[-1], dtype=jnp.int32)
    in_range = position[None, None, None, :] < valid_rows[:, None, None, None]
    scores = jnp.where(in_range, scores, NEGATIVE_FILL)
    maxima = jnp.max(scores, axis=-1)
    softmax_terms = jnp.where(in_range, jnp.exp(scores - maxima[..., None]), 0.0)
    totals = jnp.sum(softmax_terms, axis=-1)
    weighted = jnp.einsum(
        "nqhp,nhsp->nqhs",
        softmax_terms.astype(jnp.bfloat16),
        slot_values,
        preferred_element_type=jnp.float32,
    )
    return (maxima, totals, weighted)


def combine_blocks(maxima, totals, weighted, onehot):
    owned = onehot.astype(jnp.float32)
    is_live = jnp.sum(owned, axis=1) > 0.5
    masked_max = jnp.where(onehot[:, :, None, None], maxima[:, None, :, :], NEGATIVE_FILL)
    request_max = jnp.max(masked_max, axis=0)
    owner_max = jnp.einsum("nr,rqh->nqh", owned, request_max, precision=lax.Precision.HIGHEST)
    factor = jnp.exp(jnp.where(is_live[:, None, None], maxima - owner_max, NEGATIVE_FILL))
    denominator = jnp.einsum("nr,nqh->rqh", owned, factor * totals, precision=lax.Precision.HIGHEST)
    numerator = jnp.einsum(
        "nr,nqhs->rqhs", owned, factor[..., None] * weighted, precision=lax.Precision.HIGHEST
    )
    return (numerator / denominator[..., None]).astype(jnp.bfloat16)


def layer_norm(summand):
    average = jnp.mean(summand, axis=-1, keepdims=True)
    centred = summand - average
    variance = jnp.mean(centred * centred, axis=-1, keepdims=True)
    return centred * lax.rsqrt(variance + EPSILON)


def local(hist_len, queries, history_keys, cached_history_values, gain_mix, w_up, w_down, gain_out):
    group_size = lax.axis_size(("batch", "hidden"))
    my_index = lax.axis_index(("batch", "hidden"))
    head_size = MODEL_WIDTH // TOKEN_COUNT
    local_heads = history_keys.shape[1] // head_size
    slot_count = history_keys.shape[0]
    score_scale = head_size ** (-0.5)
    query_heads = queries.reshape(TOKEN_COUNT, local_heads, head_size)
    all_lengths = hist_len.reshape(group_size, REQ_DEV)
    peer_ids = jnp.arange(group_size, dtype=jnp.int32)
    mine_hot = peer_ids == my_index
    own_lengths = jnp.sum(jnp.where(mine_hot[:, None], all_lengths, 0), axis=0)
    onehot, valid_rows = slot_layout(own_lengths, slot_count, BLOCK_POSITIONS)
    slot_keys = history_keys.reshape(slot_count, local_heads, head_size, BLOCK_POSITIONS)
    slot_values = cached_history_values.reshape(slot_count, local_heads, head_size, BLOCK_POSITIONS)
    maxima, totals, weighted = block_partials(
        query_heads, slot_keys, slot_values, valid_rows, score_scale
    )
    attended = combine_blocks(maxima, totals, weighted, onehot)
    unmixed = lax.all_to_all(
        attended.reshape(REQ_DEV, TOKEN_COUNT, local_heads * head_size),
        "token",
        split_axis=1,
        concat_axis=2,
        tiled=True,
    )
    mixed_rows = jnp.transpose(attended, (0, 2, 1, 3)).reshape(
        REQ_DEV, local_heads, TOKEN_COUNT * head_size
    )
    joined = mixed_rows.astype(jnp.float32) + unmixed.astype(jnp.float32)
    normed = (layer_norm(joined) * gain_mix).astype(jnp.bfloat16)
    lifted = jnp.einsum(
        "ntd,tdf->ntf",
        lax.all_gather(normed, "hidden", axis=0, tiled=True),
        w_up,
        preferred_element_type=jnp.float32,
    )
    activated = jax.nn.gelu(lifted, approximate=False).astype(jnp.bfloat16)
    partial_sums = jnp.einsum("ntf,tfd->ntd", activated, w_down, preferred_element_type=jnp.float32)
    summed = sent_and_summed(partial_sums.astype(jnp.bfloat16), "hidden", 0)
    return (layer_norm(summed + normed.astype(jnp.float32)) * gain_out).astype(jnp.bfloat16)


def solution(mesh):
    return jax.shard_map(
        local,
        mesh=mesh,
        in_specs=(
            P(),
            P(None, "token"),
            P(("batch", "hidden"), "token", None),
            P(("batch", "hidden"), "token", None),
            P(),
            P("token", None, "hidden"),
            P("token", "hidden", None),
            P(),
        ),
        out_specs=P(("batch", "hidden"), "token", None),
        check_vma=False,
    )
```

profile of v0, /device:TPU:2, one launch (start us, length us, event | category | flops | bytes accessed | tf_op | source)
XLA Modules:
  0.0 88.5 jit_solution(1204152583943687451)
XLA Ops:
  0.0 0.0 copy-start
  0.0 0.9 reshape.733
  0.9 0.1 select_reduce_fusion.3
  1.0 0.1 copy.35
  1.1 0.1 reduce-window.7
  1.1 0.1 reduce.12
  1.2 0.1 convert_reduce_fusion.2
  1.4 0.1 select_reduce_fusion.1
  1.5 0.1 iota_compare_fusion
  1.6 0.0 copy-done
  1.6 1.3 %bitcast_reduce_fusion = (f32[96,32]{1,0:T(8,128)S(1)}, f32[1,96,128,32]{2,3,1,0:T(8,128)S(1)}) fusion(bf16[96,48,128]{2,1,0:T(8,128)(2,1)S(1)} %copy-done, bf16[32,48]{1,0:T(8,128)(2,1)} %param.9, pred[96,128]{1,0:T(8,128)(4,1)S(1)} %iota_compare_fusion), kind=kOutput, calls=%fused_computation.4 | convolution fusion | flops 38925312 | bytes 2780160 | tf_op jit(solution)/shard_map/qhs,nhsp->nqhp/dot_general | solution.py:42
  2.9 0.1 copy.37
  3.0 1.0 %fusion.5 = f32[96,32]{1,0:T(8,128)S(1)} fusion(f32[1,96,128,32]{2,3,1,0:T(8,128)S(1)} %get-tuple-element.10, f32[96,32]{1,0:T(8,128)S(1)} %get-tuple-element.9, pred[96,128]{1,0:T(8,128)(4,1)S(1)} %iota_compare_fusion), kind=kLoop, calls=%fused_computation.11 | loop fusion | flops 1176576 | bytes 1609728 | tf_op jit(solution)/shard_map/reduce_sum | solution.py:50
  4.0 0.1 copy.40
  4.0 0.2 select_reduce_fusion
  4.3 0.2 fusion.17
  4.5 0.1 copy.38
  4.6 0.1 fusion.83
  4.7 2.1 %fusion = f32[96,32,48]{2,1,0:T(8,128)S(1)} fusion(bf16[96,48,128]{2,1,0:T(8,128)(2,1)} %param.11, f32[1,96,128,32]{2,3,1,0:T(8,128)S(1)} %get-tuple-element.10, f32[96,32]{1,0:T(8,128)S(1)} %get-tuple-element.9, f32[96,32]{1,0:T(8,128)S(1)} %copy.38, pred[96,128]{1,0:T(8,128)(4,1)S(1)} %iota_compare_fusion), kind=kOutput, calls=%fused_computation.2 | convolution fusion | flops 39075840 | bytes 3379200 | tf_op jit(solution)/shard_map/nqhp,nhsp->nqhs/dot_general | solution.py:51
  6.8 1.6 %fusion.10 = bf16[32,32,48]{2,0,1:T(8,128)(2,1)S(1)} fusion(f32[96,32,48]{2,1,0:T(8,128)S(1)} %fusion, f32[32,32]{0,1:T(8,128)S(1)} %fusion.83, s32[96]{0:T(128)S(1)} %convert_reduce_fusion.2), kind=kOutput, calls=%fused_computation.14 | convolution fusion | flops 56724480 | bytes 692608 | tf_op jit(solution)/shard_map/nr,nqhs->rqhs/dot_general | solution.py:68
  8.4 0.4 reshape.745
  8.7 22.2 %all_to_all.14 = bf16[32,2,768]{2,1,0:T(2,128)(2,1)S(1)} all-to-all(bf16[32,2,768]{2,1,0:T(2,128)(2,1)S(1)} %reshape.745), channel_id=1, replica_groups=mesh['batch'=2,'token'=32,'hidden'=8] {'token'}, dimensions={0} | all-to-all | bytes 196608 | tf_op jit(solution)/shard_map/all_to_all | solution.py:100
  31.0 0.2 reshape.746
  31.2 0.0 copy-start.1
  31.2 0.2 fusion.123
  31.5 0.3 copy.42
  31.8 0.3 add.108
  32.0 0.2 multiply_reduce_fusion.1
  32.3 0.0 copy-done.1
  32.3 0.1 multiply_convert_fusion.2
  32.4 27.8 %all_gather.3 = bf16[256,1,1536]{2,0,1:T(8,128)(2,1)S(1)} all-gather(bf16[32,1,1536]{2,0,1:T(8,128)(2,1)S(1)} %multiply_convert_fusion.2), channel_id=1, replica_groups=mesh['batch'=2,'token'=32,'hidden'=8] {'hidden'}, dimensions={0}, use_global_device_ids=true | all-gather | bytes 884736 | tf_op jit(solution)/shard_map/all_gather | solution.py:114
  60.2 4.4 %convolution_convert_fusion = bf16[256,1536]{1,0:T(8,128)(2,1)} fusion(bf16[1,384,1536]{2,1,0:T(8,128)(2,1)} %param.14, bf16[1,1536,384]{2,1,0:T(8,128)(2,1)} %param.13, bf16[256,1,1536]{2,0,1:T(8,128)(2,1)S(1)} %all_gather.3), kind=kOutput, calls=%fused_computation | convolution fusion | flops 610762752 | bytes 3932160 | tf_op jit(solution)/shard_map/ntf,tfd->ntd/dot_general | solution.py:119
  64.6 5.2 %all-to-all-start.1 = ((bf16[8,32,1,1536]{3,1,2,0:T(8,128)(2,1)}), bf16[8,32,1,1536]{3,1,2,0:T(8,128)(2,1)S(1)}, u32[]{:S(2)}, u32[]{:S(2)}) async-start(bf16[8,32,1,1536]{3,1,2,0:T(8,128)(2,1)} %bitcast.162), calls=%async_computation.1 | async-start | bytes 1572864 | tf_op jit(solution)/shard_map/all_to_all | solution.py:22
  69.8 0.1 mul.216
  69.9 0.0 copy-start.2
  69.9 16.8 %all-to-all-done.1 = bf16[8,32,1,1536]{3,1,2,0:T(8,128)(2,1)S(1)} async-done(((bf16[8,32,1,1536]{3,1,2,0:T(8,128)(2,1)}), bf16[8,32,1,1536]{3,1,2,0:T(8,128)(2,1)S(1)}, u32[]{:S(2)}, u32[]{:S(2)}) %all-to-all-start.1) | async-done | bytes 786464 | tf_op jit(solution)/shard_map/all_to_all | solution.py:22
  86.7 0.1 convert_reduce_fusion
  86.8 0.2 reduce_sum.113
  87.0 0.5 fusion.24
  87.5 0.2 multiply_reduce_fusion
  87.7 0.0 copy-done.2
  87.7 0.8 multiply_convert_fusion.1
  (11 shorter events, 0.1 us)
Async XLA Ops:
  0.0 1.6 %copy-start = (bf16[96,48,128]{2,1,0:T(8,128)(2,1)S(1)}, bf16[96,48,128]{2,1,0:T(8,128)(2,1)}, u32[]{:S(2)}) copy-start(bf16[96,48,128]{2,1,0:T(8,128)(2,1)} %param.10) | copy-start | bytes 3538948
  31.2 1.0 %copy-start.1 = (f32[1536]{0:T(1024)S(1)}, f32[1536]{0:T(1024)}, u32[]{:S(2)}) copy-start(f32[1536]{0:T(1024)} %param.12) | copy-start | bytes 18436
  64.6 22.1 %all-to-all-start.1 = ((bf16[8,32,1,1536]{3,1,2,0:T(8,128)(2,1)}), bf16[8,32,1,1536]{3,1,2,0:T(8,128)(2,1)S(1)}, u32[]{:S(2)}, u32[]{:S(2)}) async-start(bf16[8,32,1,1536]{3,1,2,0:T(8,128)(2,1)} %bitcast.162), calls=%async_computation.1 | async-start | bytes 1572864 | tf_op jit(solution)/shard_map/all_to_all | solution.py:22
  69.9 17.8 %copy-start.2 = (f32[1536]{0:T(1024)S(1)}, f32[1536]{0:T(1024)}, u32[]{:S(2)}) copy-start(f32[1536]{0:T(1024)} %param.15) | copy-start | bytes 18436
where the time goes:
time: 88.8 us; the launch traced here: 88.5 us
  blocking collectives  50.1 us (56%)
  waiting for transfers between devices  16.8 us (19%)
  matrix products  9.73 us (11%)
  starting transfers between devices  5.24 us (6%)
  other arithmetic  3.89 us (4%)
  local copies, waits for them, and re-layouts  2.65 us (3%)
    all_gather x1, blocking collectives, local(): lax.all_gather(normed, 'hidden', axis=0, tiled=True)  27.8 us
    all_to_all x1, blocking collectives, local(): lax.all_to_all(attended.reshape(REQ_DEV, TOKEN_COUNT, local_heads * head_...  22.2 us
    all_to_all x1, waiting for transfers between devices, sent_and_summed(): parts = lax.all_to_all(in_blocks(x, dim, length), axis, 0, 0, tiled=True)  16.8 us
    all_to_all x1, starting transfers between devices, sent_and_summed(): parts = lax.all_to_all(in_blocks(x, dim, length), axis, 0, 0, tiled=True)  5.24 us
    dot_general x1, matrix products, local(): jnp.einsum('ntf,tfd->ntd', activated, w_down, preferred_element_type=jnp....  4.37 us
    dot_general x1, matrix products, block_partials(): jnp.einsum('nqhp,nhsp->nqhs', softmax_terms.astype(jnp.bfloat16), slot_va...  2.12 us
  transfers between devices with their start and end apart: 1, of which 1 were waited for; matrix products, arithmetic and copies ran while one was open for 0% of the time, Pallas kernels for 0%

commit v1 on v0

--- a/solution.py
+++ b/solution.py
@@ -9,6 +9,25 @@
 REQ_DEV = 32
 EPSILON = 1e-05
 NEGATIVE_FILL = -1e30
+
+
+def panel_view(vec):
+    state_now = lax.axis_size("hidden")
+    a_next = lax.axis_index("hidden")
+    finding, z, newest = (state_now, a_next, vec.shape[0])
+    column = [(b, (b + 1) % finding) for b in range(finding)]
+    res = jnp.zeros((*vec.shape[:0], finding * newest, *vec.shape[1:]), vec.dtype)
+    parts_seen = [(b, (b - 1) % finding) for b in range(finding)]
+    v_next = fresh = vec
+    placed = finding // 2
+    res = lax.dynamic_update_slice_in_dim(res, vec, z * newest, axis=0)
+    for ix in range(1, placed + 1):
+        v_next = lax.ppermute(v_next, "hidden", column)
+        res = lax.dynamic_update_slice_in_dim(res, v_next, (z - ix) % finding * newest, axis=0)
+        if ix < finding - placed:
+            fresh = lax.ppermute(fresh, "hidden", parts_seen)
+            res = lax.dynamic_update_slice_in_dim(res, fresh, (z + ix) % finding * newest, axis=0)
+    return res
 
 
 def in_blocks(x, dim, length):
@@ -110,10 +129,7 @@
     joined = mixed_rows.astype(jnp.float32) + unmixed.astype(jnp.float32)
     normed = (layer_norm(joined) * gain_mix).astype(jnp.bfloat16)
     lifted = jnp.einsum(
-        "ntd,tdf->ntf",
-        lax.all_gather(normed, "hidden", axis=0, tiled=True),
-        w_up,
-        preferred_element_type=jnp.float32,
+        "ntd,tdf->ntf", panel_view(normed), w_up, preferred_element_type=jnp.float32
     )
     activated = jax.nn.gelu(lifted, approximate=False).astype(jnp.bfloat16)
     partial_sums = jnp.einsum("ntf,tfd->ntd", activated, w_down, preferred_element_type=jnp.float32)

time: 88.8 us -> 95.4 us (1.074)
  blocking collectives: 50.1 us -> 0 us
  starting transfers between devices: 5.24 us -> 43.6 us
  waiting for transfers between devices: 16.8 us -> 33.5 us
  local copies, waits for them, and re-layouts: 2.65 us -> 3.7 us
    all_gather x1 -> x0, blocking collectives: 27.8 us -> none  [local(): lax.all_gather(normed, 'hidden', axis=0, tiled=True)]
    ppermute x0 -> x7, starting transfers between devices: none -> 23.3 us  [the longest x3 14 us: panel_view(): fresh = lax.ppermute(fresh, 'hidden', parts_seen)]
    all_to_all x1 -> x0, blocking collectives: 22.2 us -> none  [local(): lax.all_to_all(attended.reshape(REQ_DEV, TOKEN_COUNT, local_heads * head_...]
    all_to_all x0 -> x1, starting transfers between devices: none -> 13.5 us  [local(): lax.all_to_all(attended.reshape(REQ_DEV, TOKEN_COUNT, local_heads * head_...]
    all_to_all x0 -> x1, waiting for transfers between devices: none -> 8.84 us  [local(): lax.all_to_all(attended.reshape(REQ_DEV, TOKEN_COUNT, local_heads * head_...]
    ppermute x0 -> x7, waiting for transfers between devices: none -> 7.43 us  [the longest x4 7.42 us: panel_view(): v_next = lax.ppermute(v_next, 'hidden', column)]
    all_to_all x1, starting transfers between devices: 5.24 us -> 6.85 us  [sent_and_summed(): parts = lax.all_to_all(in_blocks(x, dim, length), axis, 0, 0, tiled=True)]
  transfers between devices with their start and end apart: 1 -> 9, of which waited for: 1 -> 6; matrix products, arithmetic and copies ran while one was open for 0% -> 0% of each run, Pallas kernels for 0% -> 0%
where the time goes in v1:
time: 95.4 us; the launch traced here: 94.9 us
  starting transfers between devices  43.6 us (46%)
  waiting for transfers between devices  33.5 us (35%)
  matrix products  9.71 us (10%)
  other arithmetic  3.98 us (4%)
  local copies, waits for them, and re-layouts  3.7 us (4%)
    all_to_all x1, waiting for transfers between devices, sent_and_summed(): parts = lax.all_to_all(in_blocks(x, dim, length), axis, 0, 0, tiled=True)  17.2 us
    ppermute x3, starting transfers between devices, panel_view(): fresh = lax.ppermute(fresh, 'hidden', parts_seen)  14 us
    all_to_all x1, starting transfers between devices, local(): lax.all_to_all(attended.reshape(REQ_DEV, TOKEN_COUNT, local_heads * head_...  13.5 us
    ppermute x4, starting transfers between devices, panel_view(): v_next = lax.ppermute(v_next, 'hidden', column)  9.32 us
    all_to_all x1, waiting for transfers between devices, local(): lax.all_to_all(attended.reshape(REQ_DEV, TOKEN_COUNT, local_heads * head_...  8.84 us
    ppermute x4, waiting for transfers between devices, panel_view(): v_next = lax.ppermute(v_next, 'hidden', column)  7.42 us
    all_to_all x1, starting transfers between devices, sent_and_summed(): parts = lax.all_to_all(in_blocks(x, dim, length), axis, 0, 0, tiled=True)  6.85 us
    dot_general x1, matrix products, local(): jnp.einsum('ntf,tfd->ntd', activated, w_down, preferred_element_type=jnp....  4.37 us
  transfers between devices with their start and end apart: 9, of which 6 were waited for; matrix products, arithmetic and copies ran while one was open for 0% of the time, Pallas kernels for 0%

profile of v1, /device:TPU:2, one launch (start us, length us, event | category | flops | bytes accessed | tf_op | source)
XLA Modules:
  0.0 94.9 jit_solution(12374574574263334846)
XLA Ops:
  0.0 0.0 copy-start
  0.0 0.9 reshape.775
  0.9 0.1 select_reduce_fusion.3
  1.0 0.1 copy.37
  1.1 0.1 reduce-window.7
  1.1 0.1 reduce.12
  1.3 0.1 convert_reduce_fusion.2
  1.4 0.1 select_reduce_fusion.1
  1.5 0.1 iota_compare_fusion
  1.6 0.0 copy-done
  1.6 1.3 %bitcast_reduce_fusion = (f32[96,32]{1,0:T(8,128)S(1)}, f32[1,96,128,32]{2,3,1,0:T(8,128)S(1)}) fusion(bf16[96,48,128]{2,1,0:T(8,128)(2,1)S(1)} %copy-done, bf16[32,48]{1,0:T(8,128)(2,1)} %param.9, pred[96,128]{1,0:T(8,128)(4,1)S(1)} %iota_compare_fusion), kind=kOutput, calls=%fused_computation.4 | convolution fusion | flops 38925312 | bytes 2780160 | tf_op jit(solution)/shard_map/qhs,nhsp->nqhp/dot_general | solution.py:61
  2.9 0.1 copy.39
  3.0 1.0 %fusion.5 = f32[96,32]{1,0:T(8,128)S(1)} fusion(f32[1,96,128,32]{2,3,1,0:T(8,128)S(1)} %get-tuple-element.10, f32[96,32]{1,0:T(8,128)S(1)} %get-tuple-element.9, pred[96,128]{1,0:T(8,128)(4,1)S(1)} %iota_compare_fusion), kind=kLoop, calls=%fused_computation.11 | loop fusion | flops 1176576 | bytes 1609728 | tf_op jit(solution)/shard_map/reduce_sum | solution.py:69
  4.0 0.1 copy.42
  4.0 0.2 select_reduce_fusion
  4.2 0.2 fusion.17
  4.5 0.1 copy.40
  4.6 0.1 fusion.77
  4.7 2.1 %fusion = f32[96,32,48]{2,1,0:T(8,128)S(1)} fusion(bf16[96,48,128]{2,1,0:T(8,128)(2,1)} %param.11, f32[1,96,128,32]{2,3,1,0:T(8,128)S(1)} %get-tuple-element.10, f32[96,32]{1,0:T(8,128)S(1)} %get-tuple-element.9, f32[96,32]{1,0:T(8,128)S(1)} %copy.40, pred[96,128]{1,0:T(8,128)(4,1)S(1)} %iota_compare_fusion), kind=kOutput, calls=%fused_computation.2 | convolution fusion | flops 39075840 | bytes 3379200 | tf_op jit(solution)/shard_map/nqhp,nhsp->nqhs/dot_general | solution.py:70
  6.8 1.6 %fusion.10 = bf16[32,32,48]{2,0,1:T(8,128)(2,1)S(1)} fusion(f32[96,32,48]{2,1,0:T(8,128)S(1)} %fusion, f32[32,32]{0,1:T(8,128)S(1)} %fusion.77, s32[96]{0:T(128)S(1)} %convert_reduce_fusion.2), kind=kOutput, calls=%fused_computation.14 | convolution fusion | flops 56724480 | bytes 692608 | tf_op jit(solution)/shard_map/nr,nqhs->rqhs/dot_general | solution.py:87
  8.4 1.0 %reshape.793 = bf16[32,2,768]{2,1,0:T(2,128)(2,1)} reshape(bf16[32,32,48]{2,1,0:T(8,128)(2,1)S(1)} %bitcast.167) | data formatting | bytes 196608
  9.4 13.5 %all-to-all-start = ((bf16[32,2,768]{2,1,0:T(2,128)(2,1)}), bf16[32,2,768]{2,1,0:T(2,128)(2,1)S(1)}, u32[]{:S(2)}, u32[]{:S(2)}) async-start(bf16[32,2,768]{2,1,0:T(2,128)(2,1)} %reshape.793), calls=%async_computation | async-start | bytes 196608 | tf_op jit(solution)/shard_map/all_to_all | solution.py:119
  23.0 8.8 %all-to-all-done = bf16[32,2,768]{2,1,0:T(2,128)(2,1)S(1)} async-done(((bf16[32,2,768]{2,1,0:T(2,128)(2,1)}), bf16[32,2,768]{2,1,0:T(2,128)(2,1)S(1)}, u32[]{:S(2)}, u32[]{:S(2)}) %all-to-all-start) | async-done | bytes 98336 | tf_op jit(solution)/shard_map/all_to_all | solution.py:119
  31.8 0.2 reshape.794
  32.1 0.2 fusion.117
  32.3 0.0 copy-start.1
  32.3 0.3 copy.44
  32.6 0.3 add.172
  32.9 0.3 add.171
  33.1 0.2 multiply_reduce_fusion.1
  33.3 0.0 copy-done.1
  33.3 0.1 multiply_convert_fusion.2
  33.4 3.5 %collective-permute-start = (bf16[32,1,1536]{2,0,1:T(8,128)(2,1)S(1)}, bf16[32,1,1536]{2,0,1:T(8,128)(2,1)S(1)}, u32[]{:S(2)}, u32[]{:S(2)}) collective-permute-start(bf16[32,1,1536]{2,0,1:T(8,128)(2,1)S(1)} %multiply_convert_fusion.2), channel_id=1, source_target_pairs={{0,1},{1,2},{2,3},{3,4},{4,5},{5,6},{6,7},{7,0},{8,9},{9,10},{10,1... | collective-permute-start | bytes 294920 | tf_op jit(solution)/shard_map/ppermute | solution.py:25
  36.9 3.8 %collective-permute-start.1 = (bf16[32,1,1536]{2,0,1:T(8,128)(2,1)S(1)}, bf16[32,1,1536]{2,0,1:T(8,128)(2,1)S(1)}, u32[]{:S(2)}, u32[]{:S(2)}) collective-permute-start(bf16[32,1,1536]{2,0,1:T(8,128)(2,1)S(1)} %multiply_convert_fusion.2), channel_id=1, source_target_pairs={{0,7},{1,0},{2,1},{3,2},{4,3},{5,4},{6,5},{7,6},{8,15},{9,8},{10,9... | collective-permute-start | bytes 294920 | tf_op jit(solution)/shard_map/ppermute | solution.py:28
  40.8 0.1 broadcast.494
  40.8 0.1 fusion.76
  40.9 0.5 collective-permute-done
  41.4 2.0 %collective-permute-start.2 = (bf16[32,1,1536]{2,0,1:T(8,128)(2,1)S(1)}, bf16[32,1,1536]{2,0,1:T(8,128)(2,1)S(1)}, u32[]{:S(2)}, u32[]{:S(2)}) collective-permute-start(bf16[32,1,1536]{2,0,1:T(8,128)(2,1)S(1)} %collective-permute-done), channel_id=1, source_target_pairs={{0,1},{1,2},{2,3},{3,4},{4,5},{5,6},{6,7},{7,0},{8,9},{9,10},{10,1... | collective-permute-start | bytes 294920 | tf_op jit(solution)/shard_map/ppermute | solution.py:25
  43.4 0.0 collective-permute-done.1
  43.4 5.0 %collective-permute-start.3 = (bf16[32,1,1536]{2,0,1:T(8,128)(2,1)S(1)}, bf16[32,1,1536]{2,0,1:T(8,128)(2,1)S(1)}, u32[]{:S(2)}, u32[]{:S(2)}) collective-permute-start(bf16[32,1,1536]{2,0,1:T(8,128)(2,1)S(1)} %collective-permute-done.1), channel_id=1, source_target_pairs={{0,7},{1,0},{2,1},{3,2},{4,3},{5,4},{6,5},{7,6},{8,15},{9,8},{10,9... | collective-permute-start | bytes 294920 | tf_op jit(solution)/shard_map/ppermute | solution.py:28
  48.5 0.6 collective-permute-done.2
  49.1 1.9 %collective-permute-start.4 = (bf16[32,1,1536]{2,0,1:T(8,128)(2,1)S(1)}, bf16[32,1,1536]{2,0,1:T(8,128)(2,1)S(1)}, u32[]{:S(2)}, u32[]{:S(2)}) collective-permute-start(bf16[32,1,1536]{2,0,1:T(8,128)(2,1)S(1)} %collective-permute-done.2), channel_id=1, source_target_pairs={{0,1},{1,2},{2,3},{3,4},{4,5},{5,6},{6,7},{7,0},{8,9},{9,10},{10,1... | collective-permute-start | bytes 294920 | tf_op jit(solution)/shard_map/ppermute | solution.py:25
  51.0 0.0 collective-permute-done.3
  51.1 5.1 %collective-permute-start.5 = (bf16[32,1,1536]{2,0,1:T(8,128)(2,1)S(1)}, bf16[32,1,1536]{2,0,1:T(8,128)(2,1)S(1)}, u32[]{:S(2)}, u32[]{:S(2)}) collective-permute-start(bf16[32,1,1536]{2,0,1:T(8,128)(2,1)S(1)} %collective-permute-done.3), channel_id=1, source_target_pairs={{0,7},{1,0},{2,1},{3,2},{4,3},{5,4},{6,5},{7,6},{8,15},{9,8},{10,9... | collective-permute-start | bytes 294920 | tf_op jit(solution)/shard_map/ppermute | solution.py:28
  56.2 0.6 collective-permute-done.4
  56.8 1.9 %collective-permute-start.6 = (bf16[32,1,1536]{2,0,1:T(8,128)(2,1)S(1)}, bf16[32,1,1536]{2,0,1:T(8,128)(2,1)S(1)}, u32[]{:S(2)}, u32[]{:S(2)}) collective-permute-start(bf16[32,1,1536]{2,0,1:T(8,128)(2,1)S(1)} %collective-permute-done.4), channel_id=1, source_target_pairs={{0,1},{1,2},{2,3},{3,4},{4,5},{5,6},{6,7},{7,0},{8,9},{9,10},{10,1... | collective-permute-start | bytes 294920 | tf_op jit(solution)/shard_map/ppermute | solution.py:25
  58.8 0.0 collective-permute-done.5
  58.8 5.7 %collective-permute-done.6 = bf16[32,1,1536]{2,0,1:T(8,128)(2,1)S(1)} collective-permute-done((bf16[32,1,1536]{2,0,1:T(8,128)(2,1)S(1)}, bf16[32,1,1536]{2,0,1:T(8,128)(2,1)S(1)}, u32[]{:S(2)}, u32[]{:S(2)}) %collective-permute-start.6) | collective-permute-done | bytes 98336 | tf_op jit(solution)/shard_map/ppermute | solution.py:25
  64.6 4.4 %convolution_convert_fusion = bf16[256,1536]{1,0:T(8,128)(2,1)} fusion(bf16[1,384,1536]{2,1,0:T(8,128)(2,1)} %param.14, bf16[256,1536]{1,0:T(8,128)(2,1)S(1)} %bitcast_dynamic-update-slice_fusion, bf16[1,1536,384]{2,1,0:T(8,128)(2,1)} %param.13), kind=kOutput, calls=%fused_computation | convolution fusion | flops 610762752 | bytes 3932160 | tf_op jit(solution)/shard_map/ntf,tfd->ntd/dot_general | solution.py:135
  68.9 6.8 %all-to-all-start.1 = ((bf16[8,32,1,1536]{3,1,2,0:T(8,128)(2,1)}), bf16[8,32,1,1536]{3,1,2,0:T(8,128)(2,1)S(1)}, u32[]{:S(2)}, u32[]{:S(2)}) async-start(bf16[8,32,1,1536]{3,1,2,0:T(8,128)(2,1)} %bitcast.168), calls=%async_computation.1 | async-start | bytes 1572864 | tf_op jit(solution)/shard_map/all_to_all | solution.py:41
  75.8 0.1 mul.262
  75.9 0.0 copy-start.2
  75.9 17.2 %all-to-all-done.1 = bf16[8,32,1,1536]{3,1,2,0:T(8,128)(2,1)S(1)} async-done(((bf16[8,32,1,1536]{3,1,2,0:T(8,128)(2,1)}), bf16[8,32,1,1536]{3,1,2,0:T(8,128)(2,1)S(1)}, u32[]{:S(2)}, u32[]{:S(2)}) %all-to-all-start.1) | async-done | bytes 786464 | tf_op jit(solution)/shard_map/all_to_all | solution.py:41
  93.1 0.1 convert_reduce_fusion
  93.2 0.2 reduce_sum.113
  93.4 0.5 fusion.23
  93.9 0.2 multiply_reduce_fusion
  94.2 0.0 copy-done.2
  94.2 0.8 multiply_convert_fusion.1
  (18 shorter events, 0.2 us)
Async XLA Ops:
  0.0 1.6 %copy-start = (bf16[96,48,128]{2,1,0:T(8,128)(2,1)S(1)}, bf16[96,48,128]{2,1,0:T(8,128)(2,1)}, u32[]{:S(2)}) copy-start(bf16[96,48,128]{2,1,0:T(8,128)(2,1)} %param.10) | copy-start | bytes 3538948
  9.4 22.4 %all-to-all-start = ((bf16[32,2,768]{2,1,0:T(2,128)(2,1)}), bf16[32,2,768]{2,1,0:T(2,128)(2,1)S(1)}, u32[]{:S(2)}, u32[]{:S(2)}) async-start(bf16[32,2,768]{2,1,0:T(2,128)(2,1)} %reshape.793), calls=%async_computation | async-start | bytes 196608 | tf_op jit(solution)/shard_map/all_to_all | solution.py:119
  32.3 1.1 %copy-start.1 = (f32[1536]{0:T(1024)S(1)}, f32[1536]{0:T(1024)}, u32[]{:S(2)}) copy-start(f32[1536]{0:T(1024)} %param.12) | copy-start | bytes 18436
  33.4 8.0 %collective-permute-start = (bf16[32,1,1536]{2,0,1:T(8,128)(2,1)S(1)}, bf16[32,1,1536]{2,0,1:T(8,128)(2,1)S(1)}, u32[]{:S(2)}, u32[]{:S(2)}) collective-permute-start(bf16[32,1,1536]{2,0,1:T(8,128)(2,1)S(1)} %multiply_convert_fusion.2), channel_id=1, source_target_pairs={{0,1},{1,2},{2,3},{3,4},{4,5},{5,6},{6,7},{7,0},{8,9},{9,10},{10,1... | collective-permute-start | bytes 294920 | tf_op jit(solution)/shard_map/ppermute | solution.py:25
  36.9 6.5 %collective-permute-start.1 = (bf16[32,1,1536]{2,0,1:T(8,128)(2,1)S(1)}, bf16[32,1,1536]{2,0,1:T(8,128)(2,1)S(1)}, u32[]{:S(2)}, u32[]{:S(2)}) collective-permute-start(bf16[32,1,1536]{2,0,1:T(8,128)(2,1)S(1)} %multiply_convert_fusion.2), channel_id=1, source_target_pairs={{0,7},{1,0},{2,1},{3,2},{4,3},{5,4},{6,5},{7,6},{8,15},{9,8},{10,9... | collective-permute-start | bytes 294920 | tf_op jit(solution)/shard_map/ppermute | solution.py:28
  41.4 7.7 %collective-permute-start.2 = (bf16[32,1,1536]{2,0,1:T(8,128)(2,1)S(1)}, bf16[32,1,1536]{2,0,1:T(8,128)(2,1)S(1)}, u32[]{:S(2)}, u32[]{:S(2)}) collective-permute-start(bf16[32,1,1536]{2,0,1:T(8,128)(2,1)S(1)} %collective-permute-done), channel_id=1, source_target_pairs={{0,1},{1,2},{2,3},{3,4},{4,5},{5,6},{6,7},{7,0},{8,9},{9,10},{10,1... | collective-permute-start | bytes 294920 | tf_op jit(solution)/shard_map/ppermute | solution.py:25
  43.4 7.6 %collective-permute-start.3 = (bf16[32,1,1536]{2,0,1:T(8,128)(2,1)S(1)}, bf16[32,1,1536]{2,0,1:T(8,128)(2,1)S(1)}, u32[]{:S(2)}, u32[]{:S(2)}) collective-permute-start(bf16[32,1,1536]{2,0,1:T(8,128)(2,1)S(1)} %collective-permute-done.1), channel_id=1, source_target_pairs={{0,7},{1,0},{2,1},{3,2},{4,3},{5,4},{6,5},{7,6},{8,15},{9,8},{10,9... | collective-permute-start | bytes 294920 | tf_op jit(solution)/shard_map/ppermute | solution.py:28
  49.1 7.7 %collective-permute-start.4 = (bf16[32,1,1536]{2,0,1:T(8,128)(2,1)S(1)}, bf16[32,1,1536]{2,0,1:T(8,128)(2,1)S(1)}, u32[]{:S(2)}, u32[]{:S(2)}) collective-permute-start(bf16[32,1,1536]{2,0,1:T(8,128)(2,1)S(1)} %collective-permute-done.2), channel_id=1, source_target_pairs={{0,1},{1,2},{2,3},{3,4},{4,5},{5,6},{6,7},{7,0},{8,9},{9,10},{10,1... | collective-permute-start | bytes 294920 | tf_op jit(solution)/shard_map/ppermute | solution.py:25
  51.1 7.7 %collective-permute-start.5 = (bf16[32,1,1536]{2,0,1:T(8,128)(2,1)S(1)}, bf16[32,1,1536]{2,0,1:T(8,128)(2,1)S(1)}, u32[]{:S(2)}, u32[]{:S(2)}) collective-permute-start(bf16[32,1,1536]{2,0,1:T(8,128)(2,1)S(1)} %collective-permute-done.3), channel_id=1, source_target_pairs={{0,7},{1,0},{2,1},{3,2},{4,3},{5,4},{6,5},{7,6},{8,15},{9,8},{10,9... | collective-permute-start | bytes 294920 | tf_op jit(solution)/shard_map/ppermute | solution.py:28
  56.8 7.7 %collective-permute-start.6 = (bf16[32,1,1536]{2,0,1:T(8,128)(2,1)S(1)}, bf16[32,1,1536]{2,0,1:T(8,128)(2,1)S(1)}, u32[]{:S(2)}, u32[]{:S(2)}) collective-permute-start(bf16[32,1,1536]{2,0,1:T(8,128)(2,1)S(1)} %collective-permute-done.4), channel_id=1, source_target_pairs={{0,1},{1,2},{2,3},{3,4},{4,5},{5,6},{6,7},{7,0},{8,9},{9,10},{10,1... | collective-permute-start | bytes 294920 | tf_op jit(solution)/shard_map/ppermute | solution.py:25
  68.9 24.2 %all-to-all-start.1 = ((bf16[8,32,1,1536]{3,1,2,0:T(8,128)(2,1)}), bf16[8,32,1,1536]{3,1,2,0:T(8,128)(2,1)S(1)}, u32[]{:S(2)}, u32[]{:S(2)}) async-start(bf16[8,32,1,1536]{3,1,2,0:T(8,128)(2,1)} %bitcast.168), calls=%async_computation.1 | async-start | bytes 1572864 | tf_op jit(solution)/shard_map/all_to_all | solution.py:41
  75.9 18.3 %copy-start.2 = (f32[1536]{0:T(1024)S(1)}, f32[1536]{0:T(1024)}, u32[]{:S(2)}) copy-start(f32[1536]{0:T(1024)} %param.15) | copy-start | bytes 18436
